TPU v7x, 512 devices: a whole 4x8x8 slice. The times are simulated.
512 devices in a mesh: tensor: 128 (over z, y_lo, x, core), dp: 4 (over y_hi).
Axes of the slice: x: 4, y: 8 (y_hi: 4, y_lo: 2; y = y_hi * 2 + y_lo), z: 8, core: 2. Of those that a mesh axis runs over, the one named last changes fastest.
Arguments:
- tokens: bfloat16 [1024, 4096], P(('dp', 'tensor')), parts along dimension 0, may hold values from -120 to 120
- gate_weight: bfloat16 [26624, 4096], P('tensor'), may hold values from -0.09375 to 0.09375
- up_weight: bfloat16 [26624, 4096], P('tensor'), may hold values from -0.09375 to 0.09375
- down_weight: bfloat16 [26624, 4096], P('tensor'), may hold values from -0.0390625 to 0.0390625
Outputs:
- output: bfloat16 [1024, 4096], P(('dp', 'tensor')), parts along dimension 0
There are 4 independent parts, one for each index of `dp`. A program takes and returns all parts, laid end to end along the dimension named above; an argument that names none is the same for every part. Nothing has to cross between parts.
All inputs are finite; a program needn't handle non-finite values. Where the computation divides by a largest or mean magnitude, that divisor is 1e-20 or more.
Results may differ from a plain program's by a relative error of at most 0.0065.
Values may be sent and summed in bfloat16 or wider, within the bound.
A program may use at most 64 MiB of HBM per device.

v0:
```python
import jax
import jax.numpy as jnp
from jax import lax
from jax.experimental import pallas as pl
from jax.experimental.pallas import tpu as pltpu
from jax.sharding import PartitionSpec as P

TARGET = 16.0
EPSILON = 1e-06
F32, BF16 = jnp.float32, jnp.bfloat16

D = 4096
UNITS = 208
NZ, NX, NY = 8, 4, 2
NXY = NX * NY
CHIPS = NZ * NXY
LANES = 128
NJ = D // LANES
ROWS = 2 * NJ
PITCH = ROWS + 8
CUT = 16
NEAR = (1, 7, 2, 6, 3, 5, 4)
FAR_PLANE = (6, 5, 7, 2, 4, 1, 3)
HALF = NZ // 2


def kernel(
    x_ref, wg_ref, wu_ref, wd_ref, o_ref,
    x_in, rx, fx, xs, wg, wu, wd, part, sums, sb, ra4, ra1, sb4, sb1, rb4, rb1, tmp, pk_mine, pk_z, pk_plane, pk_both,
    x_sem, load_sem, wsend, wrecv, pk_send, pk_zr, pk_pr, pk_sib,
    here_sib, ag_send, ag4_z, ag1_p, ag4_p, ag1_z,
    rs_send, rs4_p, rs1_z, rs4_z, rs1_p,
):
    me = lax.axis_index("tensor")
    core = lax.rem(me, 2)
    chip = me // 2
    z, xy = chip // NXY, lax.rem(chip, NXY)
    y, x = xy // NX, lax.rem(xy, NX)

    def plane(k):
        return lax.rem(y + k // NX, NY) * NX + lax.rem(x + lax.rem(k, NX), NX)

    def zed(k):
        return lax.rem(z + k, NZ)

    def dev(zz, pp):
        return {"tensor": (zz * NXY + pp) * 2 + core}

    sibling = {"tensor": chip * 2 + 1 - core}

    def send(src, dst, ssem, rsem, to):
        pltpu.make_async_remote_copy(src, dst, ssem, rsem, device_id=to, device_id_type=pl.DeviceIdType.MESH).start()

    def arrive(ref, sem):
        pltpu.make_async_copy(ref, ref, sem).wait()

    barrier = pltpu.get_barrier_semaphore()

    def greet(k, _):
        pl.semaphore_signal(barrier, inc=1, device_id=dev(zed(k), xy), device_id_type=pl.DeviceIdType.MESH)
        pl.semaphore_signal(barrier, inc=1, device_id=dev(z, plane(k)), device_id_type=pl.DeviceIdType.MESH)
        return 0

    lax.fori_loop(1, 8, greet, 0)
    @pl.when(core == 0)
    def _():
        pl.semaphore_signal(barrier, inc=1, device_id=sibling, device_id_type=pl.DeviceIdType.MESH)

    x_copy = pltpu.make_async_copy(x_ref, x_in, x_sem)
    x_copy.start()
    own = [(wg_ref, wg), (wu_ref, wu), (wd_ref, wd)]
    for i, (src, dst) in enumerate(own):
        pltpu.make_async_copy(src, dst.at[pl.ds(0, UNITS)], load_sem.at[i]).start()

    x_copy.wait()
    mine = x_in[...].astype(F32)
    for j in range(NJ):
        tmp[2 * j : 2 * j + 2, :] = mine[:, j * LANES : (j + 1) * LANES]
    rx[chip] = tmp[...].astype(BF16)
    pk_mine[0] = jnp.max(jnp.abs(tmp[...]), axis=0, keepdims=True)

    pl.semaphore_wait(barrier, 14 + core)

    @pl.when(core == 1)
    def _():
        pl.semaphore_signal(here_sib, inc=1, device_id=sibling, device_id_type=pl.DeviceIdType.MESH)

    low, high = pl.ds(0, CUT), pl.ds(CUT, ROWS - CUT)

    def arrive_if(here, ref, sem):
        pl.when(here)(lambda: arrive(ref, sem))

    for k in NEAR:
        send(pk_mine.at[0], pk_z.at[k], pk_send.at[0], pk_zr.at[k], dev(zed(k), xy))
    for k in NEAR:
        send(rx.at[chip, high], rx.at[chip, high], ag_send.at[0], ag4_z.at[k], dev(zed(k), xy))
    for k in FAR_PLANE:
        send(rx.at[chip, low], rx.at[chip, low], ag_send.at[1], ag1_p.at[k], dev(z, plane(k)))

    def to_plane(zz):
        block = zz * NXY + xy
        for k in FAR_PLANE:
            send(rx.at[block, high], rx.at[block, high], ag_send.at[2], ag4_p.at[zz], dev(z, plane(k)))

    def spread4(zz):
        arrive(rx.at[zz * NXY + xy, high], ag4_z.at[lax.rem(z - zz + NZ, NZ)])
        to_plane(zz)

    def spread1(p):
        block = z * NXY + plane(p)
        if p:
            arrive(rx.at[block, low], ag1_p.at[(NX - p) % NX + p // NX * NX])
        for k in NEAR[::-1]:
            send(rx.at[block, low], rx.at[block, low], ag_send.at[3], ag1_z.at[k], dev(zed(k), xy))

    early = z < HALF
    to_plane(z)
    def weights_to_sibling():
        for i, (src, dst) in enumerate(own):
            send(src, dst.at[pl.ds(UNITS, UNITS)], wsend.at[i], wrecv.at[i], sibling)

    pl.when(core == 1)(weights_to_sibling)
    for k in (1, 7):
        spread4(zed(k))

    @pl.when(core == 0)
    def _():
        pl.semaphore_wait(here_sib, 1)
        weights_to_sibling()

    for k in (2, 6):
        spread4(zed(k))
    for p in range(1, 8):
        arrive(rx.at[0, low], ag1_p.at[p])
    for k in NEAR[::-1]:
        blocks = rx.at[pl.ds(z * NXY, NXY), low]
        send(blocks, blocks, ag_send.at[3], ag1_z.at[k], dev(zed(k), xy))
    for k in (3, 5, 4):
        spread4(zed(k))

    peak = pk_mine[0]
    for k in NEAR:
        arrive(pk_z.at[k], pk_zr.at[k])
        peak = jnp.maximum(peak, pk_z[k])
    pk_mine[1] = peak
    for k in FAR_PLANE:
        send(pk_mine.at[1], pk_plane.at[k], pk_send.at[1], pk_pr.at[k], dev(z, plane(k)))

    def collect(zz, start, size):
        for b in range(NXY):
            fx[b * size : (b + 1) * size, :] = rx[zz * NXY + b, start : start + size].astype(F32)
        for j in range(size // 2):
            pair = [fx[pl.ds(2 * j + t, 8, stride=size), :] for t in range(2)]
            at = start // 2 + j
            xs[zz * 16 : (zz + 1) * 16, at * LANES : (at + 1) * LANES] = jnp.concatenate(pair, axis=0).astype(BF16)

    def contract(w, start, size):
        cols = slice(start * LANES // 2, (start + size) * LANES // 2)
        return lax.dot_general(xs[:, cols], w[:, cols], (((1,), (1,)), ((), ())), preferred_element_type=F32)

    def expand(gate, up):
        gate = gate * factor
        hidden = (gate / (1.0 + jnp.exp(-gate)) * (up * factor)).astype(BF16)
        part[...] = jnp.dot(hidden, wd[...], preferred_element_type=F32)

    def lay_out(zz, start, size):
        for j in range(start // 2, (start + size) // 2):
            for t in range(2):
                rows = part[zz * 16 + t * 8 : zz * 16 + t * 8 + 8, j * LANES : (j + 1) * LANES]
                sums[pl.ds(zz * (NXY * PITCH) + 2 * j + t, 8, stride=PITCH), :] = rows
        for b in range(NXY):
            g = zz * NXY + b
            sb[g, start : start + size] = sums[g * PITCH + start : g * PITCH + start + size, :].astype(BF16)

    def scatter1():
        for zz in range(NZ):
            lay_out(zz, 0, CUT)
        for k in NEAR[::-1]:
            send(sb.at[pl.ds(zed(k) * NXY, NXY), low], ra1.at[k], rs_send.at[1], rs1_z.at[k], dev(zed(k), xy))

    def scatter4(zz):
        lay_out(zz, CUT, ROWS - CUT)
        for k in FAR_PLANE:
            send(sb.at[zz * NXY + plane(k), high], ra4.at[zz, k - 1], rs_send.at[0], rs4_p.at[zz], dev(z, plane(k)))

    def mine_of(block, start, size):
        return sums[pl.ds(pl.multiple_of(block * PITCH + start, 8), size), :]

    def gather4(zz):
        arrive(ra4.at[zz], rs4_p.at[zz])
        total = mine_of(zz * NXY + xy, CUT, ROWS - CUT)
        for k in range(7):
            total = total + ra4[zz, k].astype(F32)

        @pl.when(z != zz)
        def _():
            k = lax.rem(zz - z + NZ, NZ)
            sb4[zz] = total.astype(BF16)
            send(sb4.at[zz], rb4.at[k], rs_send.at[2], rs4_z.at[k], dev(zz, xy))

        @pl.when(z == zz)
        def _():
            tmp[CUT:, :] = total

    def gather1():
        for k in NEAR:
            arrive(ra1.at[k], rs1_z.at[k])
        for k in (*FAR_PLANE, 0):
            p = plane(k)
            total = mine_of(z * NXY + p, 0, CUT)
            for i in NEAR:
                total = total + ra1[i, p].astype(F32)
            if k:
                sb1[k] = total.astype(BF16)
                send(sb1.at[k], rb1.at[k], rs_send.at[3], rs1_p.at[k], dev(z, p))
            else:
                tmp[:CUT, :] = total

    for zz in range(NZ):
        arrive_if(z != zz, rx.at[pl.ds(0, NXY), low], ag1_z.at[lax.rem(z - zz + NZ, NZ)])
        collect(zz, 0, CUT)
    for k in FAR_PLANE:
        arrive(pk_plane.at[k], pk_pr.at[k])
        peak = jnp.maximum(peak, pk_plane[k])
    pk_mine[2] = peak
    send(pk_mine.at[2], pk_both.at[0], pk_send.at[2], pk_sib, sibling)
    for zz in range(NZ):
        arrive(rx.at[pl.ds(0, 7), high], ag4_p.at[zz])
        collect(zz, CUT, ROWS - CUT)

    for i, (src, dst) in enumerate(own[:2]):
        pltpu.make_async_copy(src, dst.at[pl.ds(0, UNITS)], load_sem.at[i]).wait()
        arrive(dst.at[pl.ds(UNITS, UNITS)], wrecv.at[i])
    gate = contract(wg, 0, ROWS)
    up = contract(wu, 0, ROWS)
    pltpu.make_async_copy(wd_ref, wd.at[pl.ds(0, UNITS)], load_sem.at[2]).wait()
    arrive(wd.at[pl.ds(UNITS, UNITS)], wrecv.at[2])
    arrive(pk_both.at[0], pk_sib)
    top = jnp.max(jnp.maximum(peak, pk_both[0]), keepdims=True)
    factor = TARGET / (top + EPSILON)
    expand(gate, up)

    scatter1()
    for zz in range(NZ):
        scatter4(zz)

    for zz in range(HALF):
        gather4(zz)
    pl.when(early)(gather1)
    for zz in range(HALF, NZ):
        gather4(zz)
    pl.when(z >= HALF)(gather1)

    for k in NEAR:
        arrive(rb4.at[k], rs4_z.at[k])
        tmp[CUT:, :] += rb4[k].astype(F32)
    for k in FAR_PLANE:
        arrive(rb1.at[k], rs1_p.at[k])
        tmp[:CUT, :] += rb1[k].astype(F32)
    for j in range(NJ):
        o_ref[:, j * LANES : (j + 1) * LANES] = tmp[2 * j : 2 * j + 2, :].astype(BF16)

    for i, (src, dst) in enumerate(own):
        arrive(dst.at[pl.ds(UNITS, UNITS)], wsend.at[i])
    arrive(pk_z.at[pl.ds(0, 7)], pk_send.at[0])
    arrive(pk_plane.at[pl.ds(0, 7)], pk_send.at[1])
    arrive(pk_both.at[0], pk_send.at[2])
    arrive(rx.at[pl.ds(0, 7), high], ag_send.at[0])
    arrive(rx.at[pl.ds(0, 7), low], ag_send.at[1])
    arrive(rx.at[pl.ds(0, 56), high], ag_send.at[2])
    arrive(rx.at[pl.ds(0, 56), low], ag_send.at[3])
    arrive(sb.at[pl.ds(0, 56), high], rs_send.at[0])
    arrive(sb.at[pl.ds(0, 56), low], rs_send.at[1])
    arrive(sb.at[pl.ds(0, 7), high], rs_send.at[2])
    arrive(sb.at[pl.ds(0, 7), low], rs_send.at[3])


def shards(tokens, gate_weight, up_weight, down_weight):
    vmem, hbm = pl.BlockSpec(memory_space=pltpu.VMEM), pl.BlockSpec(memory_space=pl.ANY)
    dma = pltpu.SemaphoreType.DMA
    high = ROWS - CUT
    return pl.pallas_call(
        kernel,
        out_shape=jax.ShapeDtypeStruct((2, D), BF16),
        in_specs=[hbm, hbm, hbm, hbm],
        out_specs=vmem,
        scratch_shapes=[
            pltpu.VMEM((2, D), BF16),
            pltpu.VMEM((CHIPS, ROWS, LANES), BF16),
            pltpu.VMEM((NXY * ROWS, LANES), F32),
            pltpu.VMEM((2 * CHIPS, D), BF16),
            pltpu.VMEM((2 * UNITS, D), BF16),
            pltpu.VMEM((2 * UNITS, D), BF16),
            pltpu.VMEM((2 * UNITS, D), BF16),
            pltpu.VMEM((2 * CHIPS, D), F32),
            pltpu.VMEM((CHIPS * PITCH, LANES), F32),
            pltpu.VMEM((CHIPS, ROWS, LANES), BF16),
            pltpu.VMEM((NZ, 7, high, LANES), BF16),
            pltpu.VMEM((8, NXY, CUT, LANES), BF16),
            pltpu.VMEM((8, high, LANES), BF16),
            pltpu.VMEM((8, CUT, LANES), BF16),
            pltpu.VMEM((8, high, LANES), BF16),
            pltpu.VMEM((8, CUT, LANES), BF16),
            pltpu.VMEM((ROWS, LANES), F32),
            pltpu.VMEM((3, 1, LANES), F32),
            pltpu.VMEM((8, 1, LANES), F32),
            pltpu.VMEM((8, 1, LANES), F32),
            pltpu.VMEM((1, 1, LANES), F32),
            dma, dma((3,)), dma((3,)), dma((3,)), dma((3,)), dma((8,)), dma((8,)), dma,
            pltpu.SemaphoreType.REGULAR,
            dma((4,)), dma((8,)), dma((8,)), dma((8,)), dma((8,)),
            dma((4,)), dma((8,)), dma((8,)), dma((8,)), dma((8,)),
        ],
        compiler_params=pltpu.CompilerParams(collective_id=0, has_side_effects=True, vmem_limit_bytes=60 << 20),
        name="ffn",
    )(tokens, gate_weight, up_weight, down_weight)


def solution(mesh):
    placed = (P(("dp", "tensor"), None), P("tensor", None), P("tensor", None), P("tensor", None))
    return jax.shard_map(
        shards, mesh=mesh, in_specs=placed, out_specs=P(("dp", "tensor"), None), check_vma=False
    )
```

profile of v0, /device:TPU:16, one launch (start us, length us, event | category | flops | bytes accessed | tf_op | source)
XLA Modules:
  0.0 42.6 jit_solution(3118867829100590008)
XLA Ops:
  0.0 41.3 %ffn.1 = bf16[2,4096]{1,0:T(2,128)(2,1)} custom-call(bf16[2,4096]{1,0:T(2,128)(2,1)} %x_ref.1, bf16[208,4096]{1,0:T(8,128)(2,1)} %wg_ref.1, bf16[208,4096]{1,0:T(8,128)(2,1)} %wu_ref.1, bf16[208,4096]{1,0:T(8,128)(2,1)} %wd_ref.1), custom_call_target="tpu_custom_call" | custom-call | tf_op jit(solution)/shard_map/ffn/pallas_call | solution.py:282
  41.3 1.3 %copy.6 = bf16[2,4096]{1,0:T(2,128)(2,1)} copy(bf16[2,4096]{1,0:T(2,128)(2,1)} %ffn.1) | data formatting | bytes 32768
where the time goes:
time: 42.8 us; the launch traced here: 42.6 us
  Pallas kernels  41.3 us (96%)
  local copies, waits for them, and re-layouts  1.34 us (3%)
    pallas_call x1, Pallas kernels, shards(): pl.pallas_call(kernel, out_shape=jax.ShapeDtypeStruct((2, D), BF16), in_s...  41.3 us
    unnamed x1, local copies, waits for them, and re-layouts  1.34 us

commit v1 on v0

--- a/solution.py
+++ b/solution.py
@@ -56,12 +56,10 @@
 
     barrier = pltpu.get_barrier_semaphore()
 
-    def greet(k, _):
+    for k in NEAR[::-1]:
         pl.semaphore_signal(barrier, inc=1, device_id=dev(zed(k), xy), device_id_type=pl.DeviceIdType.MESH)
+    for k in FAR_PLANE:
         pl.semaphore_signal(barrier, inc=1, device_id=dev(z, plane(k)), device_id_type=pl.DeviceIdType.MESH)
-        return 0
-
-    lax.fori_loop(1, 8, greet, 0)
     @pl.when(core == 0)
     def _():
         pl.semaphore_signal(barrier, inc=1, device_id=sibling, device_id_type=pl.DeviceIdType.MESH)
@@ -86,6 +84,13 @@
         pl.semaphore_signal(here_sib, inc=1, device_id=sibling, device_id_type=pl.DeviceIdType.MESH)
 
     low, high = pl.ds(0, CUT), pl.ds(CUT, ROWS - CUT)
+
+    def each(start, stop, body):
+        def step(i, _):
+            body(i)
+            return 0
+
+        lax.fori_loop(start, stop, step, 0)
 
     def arrive_if(here, ref, sem):
         pl.when(here)(lambda: arrive(ref, sem))
@@ -152,7 +157,7 @@
         for j in range(size // 2):
             pair = [fx[pl.ds(2 * j + t, 8, stride=size), :] for t in range(2)]
             at = start // 2 + j
-            xs[zz * 16 : (zz + 1) * 16, at * LANES : (at + 1) * LANES] = jnp.concatenate(pair, axis=0).astype(BF16)
+            xs[pl.ds(pl.multiple_of(zz * 16, 16), 16), at * LANES : (at + 1) * LANES] = jnp.concatenate(pair, axis=0).astype(BF16)
 
     def contract(w, start, size):
         cols = slice(start * LANES // 2, (start + size) * LANES // 2)
@@ -166,15 +171,14 @@
     def lay_out(zz, start, size):
         for j in range(start // 2, (start + size) // 2):
             for t in range(2):
-                rows = part[zz * 16 + t * 8 : zz * 16 + t * 8 + 8, j * LANES : (j + 1) * LANES]
+                rows = part[pl.ds(pl.multiple_of(zz * 16 + t * 8, 8), 8), j * LANES : (j + 1) * LANES]
                 sums[pl.ds(zz * (NXY * PITCH) + 2 * j + t, 8, stride=PITCH), :] = rows
         for b in range(NXY):
             g = zz * NXY + b
-            sb[g, start : start + size] = sums[g * PITCH + start : g * PITCH + start + size, :].astype(BF16)
+            sb[g, start : start + size] = sums[pl.ds(pl.multiple_of(g * PITCH + start, 8), size), :].astype(BF16)
 
     def scatter1():
-        for zz in range(NZ):
-            lay_out(zz, 0, CUT)
+        each(0, NZ, lambda zz: lay_out(zz, 0, CUT))
         for k in NEAR[::-1]:
             send(sb.at[pl.ds(zed(k) * NXY, NXY), low], ra1.at[k], rs_send.at[1], rs1_z.at[k], dev(zed(k), xy))
 
@@ -216,17 +220,21 @@
             else:
                 tmp[:CUT, :] = total
 
-    for zz in range(NZ):
+    def collect1(zz):
         arrive_if(z != zz, rx.at[pl.ds(0, NXY), low], ag1_z.at[lax.rem(z - zz + NZ, NZ)])
         collect(zz, 0, CUT)
+
+    def collect4(zz):
+        arrive(rx.at[pl.ds(0, 7), high], ag4_p.at[zz])
+        collect(zz, CUT, ROWS - CUT)
+
+    each(0, NZ, collect1)
     for k in FAR_PLANE:
         arrive(pk_plane.at[k], pk_pr.at[k])
         peak = jnp.maximum(peak, pk_plane[k])
     pk_mine[2] = peak
     send(pk_mine.at[2], pk_both.at[0], pk_send.at[2], pk_sib, sibling)
-    for zz in range(NZ):
-        arrive(rx.at[pl.ds(0, 7), high], ag4_p.at[zz])
-        collect(zz, CUT, ROWS - CUT)
+    each(0, NZ, collect4)
 
     for i, (src, dst) in enumerate(own[:2]):
         pltpu.make_async_copy(src, dst.at[pl.ds(0, UNITS)], load_sem.at[i]).wait()
@@ -241,14 +249,11 @@
     expand(gate, up)
 
     scatter1()
-    for zz in range(NZ):
-        scatter4(zz)
-
-    for zz in range(HALF):
-        gather4(zz)
+    each(0, NZ, scatter4)
+
+    each(0, HALF, gather4)
     pl.when(early)(gather1)
-    for zz in range(HALF, NZ):
-        gather4(zz)
+    each(HALF, NZ, gather4)
     pl.when(z >= HALF)(gather1)
 
     for k in NEAR:

time: 42.8 us -> 42.8 us (level)
  no operation moved by 1% of the time
where the time goes in v1:
time: 42.8 us; the launch traced here: 42.6 us
  Pallas kernels  41.3 us (96%)
  local copies, waits for them, and re-layouts  1.34 us (3%)
    pallas_call x1, Pallas kernels, shards(): pl.pallas_call(kernel, out_shape=jax.ShapeDtypeStruct((2, D), BF16), in_s...  41.3 us
    unnamed x1, local copies, waits for them, and re-layouts  1.34 us

profile of v1, /device:TPU:16, one launch (start us, length us, event | category | flops | bytes accessed | tf_op | source)
XLA Modules:
  0.0 42.6 jit_solution(11426525278267180770)
XLA Ops:
  0.0 41.3 %ffn.1 = bf16[2,4096]{1,0:T(2,128)(2,1)} custom-call(bf16[2,4096]{1,0:T(2,128)(2,1)} %x_ref.1, bf16[208,4096]{1,0:T(8,128)(2,1)} %wg_ref.1, bf16[208,4096]{1,0:T(8,128)(2,1)} %wu_ref.1, bf16[208,4096]{1,0:T(8,128)(2,1)} %wd_ref.1), custom_call_target="tpu_custom_call" | custom-call | tf_op jit(solution)/shard_map/ffn/pallas_call | solution.py:287
  41.3 1.3 %copy.6 = bf16[2,4096]{1,0:T(2,128)(2,1)} copy(bf16[2,4096]{1,0:T(2,128)(2,1)} %ffn.1) | data formatting | bytes 32768
